TPU v7x, 32 devices: a whole 2x2x4 slice. The times are simulated.
32 devices in a mesh: ia: 8 (over z, y), ja: 2 (over core), ka: 2 (over x).
Axes of the slice: x: 2, y: 2, z: 4, core: 2. Of those that a mesh axis runs over, the one named last changes fastest.
Arguments:
- tensor: bfloat16 [64, 2048, 256], P('ia', 'ja', 'ka'), may hold values from -115200 to 115200
- factor_b: float32 [8, 2, 2, 64, 64], P('ia', 'ja', 'ka'), may hold values from -4.5 to 13.5
- factor_c: float32 [2, 8, 2, 8, 64], P('ka', 'ia', 'ja'), may hold values from -4.5 to 13.5
Outputs:
- factor_a: float32 [64, 64], P('ia')
- factor_b_out: float32 [8, 2, 2, 64, 64], P('ia', 'ja', 'ka')
All inputs are finite; a program needn't handle non-finite values.
Results may differ from a plain program's by a relative error of at most 0.008.
Values may be sent and summed in bfloat16 or wider, within the bound.
A program may use at most 64 MiB of HBM per device.

v0:
```python
import jax
import jax.numpy as jnp
from jax import lax
from jax.sharding import PartitionSpec as P

epsilon = 1e-06


def solve_normal(gram_mat, rhs_rows):
    factor_low = jnp.linalg.cholesky(gram_mat)
    return jax.scipy.linalg.cho_solve((factor_low, True), rhs_rows.T).T


def self_gram(rows_data):
    return jnp.dot(
        rows_data.T, rows_data, precision=lax.Precision.HIGHEST, preferred_element_type=jnp.float32
    )


def body(tensor, factor_b, factor_c):
    rank_cols = factor_b.shape[-1]
    own_b = factor_b.reshape(-1, rank_cols)
    own_c = factor_c.reshape(-1, rank_cols)
    rows_i, rows_j, rows_k = tensor.shape
    block_c = lax.all_gather(own_c.astype(jnp.bfloat16), ("ia", "ja"), axis=0, tiled=True)
    partial_value = jnp.einsum(
        "ijk,kr->irj", tensor, block_c, preferred_element_type=jnp.float32
    ).astype(jnp.bfloat16)
    block_b = lax.all_gather(own_b.astype(jnp.bfloat16), ("ia", "ka"), axis=0, tiled=True)
    mode_local = jnp.einsum(
        "irj,jr->ir", partial_value, block_b, preferred_element_type=jnp.float32
    )
    mode_a = lax.psum(mode_local, ("ja", "ka"))
    gram_b, gram_c = lax.psum((self_gram(own_b), self_gram(own_c)), ("ia", "ja", "ka"))
    a_new = solve_normal(gram_b * gram_c, mode_a)
    count_i = rows_i * lax.axis_size("ia")
    squares = lax.psum(jnp.sum(a_new * a_new, axis=0), "ia")
    factor_a = a_new * lax.rsqrt(squares / count_i + epsilon)
    gram_a = lax.psum(self_gram(factor_a), "ia")
    cast_a = factor_a.astype(jnp.bfloat16)
    mode_b = lax.psum_scatter(
        jnp.einsum("irj,ir->jr", partial_value, cast_a, preferred_element_type=jnp.float32),
        ("ia", "ka"),
        scatter_dimension=0,
        tiled=True,
    )
    b_new = solve_normal(gram_a * gram_c, mode_b)
    sums_b = lax.psum(jnp.sum(b_new * b_new, axis=0), ("ia", "ja", "ka"))
    count_j = rows_j * lax.axis_size("ja")
    out_rows = b_new * lax.rsqrt(sums_b / count_j + epsilon)
    return (factor_a, out_rows.reshape(factor_b.shape))


def solution(mesh):
    return jax.shard_map(
        body,
        mesh=mesh,
        in_specs=(
            P("ia", "ja", "ka"),
            P("ia", "ja", "ka", None, None),
            P("ka", "ia", "ja", None, None),
        ),
        out_specs=(P("ia", None), P("ia", "ja", "ka", None, None)),
        check_vma=False,
    )
```

profile of v0, /device:TPU:0, one launch (start us, length us, event | category | flops | bytes accessed | tf_op | source)
XLA Modules:
  0.0 279.5 jit_solution(18311145220735601781)
XLA Ops:
  7.2 0.9 bitcast_convert_fusion
  8.1 1.1 fusion.18
  9.2 0.7 bitcast_convert_fusion.1
  9.9 1.0 fusion.20
  10.9 43.8 %all_gather.7 = bf16[1024,64]{1,0:T(8,128)(2,1)S(1)} all-gather(bf16[64,64]{1,0:T(8,128)(2,1)S(1)} %bitcast_convert_fusion), channel_id=1, replica_groups=mesh['ia'=8,'ja'=2,'ka'=2] {'ia','ka'}, dimensions={0}, use_global_device_ids=true | all-gather | bytes 139264 | tf_op jit(solution)/shard_map/all_gather | solution.py:29
  54.7 0.3 copy.18
  54.9 17.2 %all_gather.6 = bf16[128,64]{1,0:T(8,128)(2,1)S(1)} all-gather(bf16[8,64]{1,0:T(8,128)(2,1)S(1)} %bitcast_convert_fusion.1), channel_id=1, replica_groups=mesh['ia'=8,'ja'=2,'ka'=2] {'ia','ja'}, dimensions={0}, use_global_device_ids=true | all-gather | bytes 17408 | tf_op jit(solution)/shard_map/all_gather | solution.py:25
  72.1 0.9 fusion
  73.0 0.9 fusion.3
  74.0 11.8 %psum.44 = f32[8,64]{0,1:T(8,128)S(1)} all-reduce(f32[8,64]{0,1:T(8,128)S(1)} %bitcast.64), channel_id=1, replica_groups=mesh['ia'=8,'ja'=2,'ka'=2] {'ja','ka'}, use_global_device_ids=true, to_apply=%region_4.6 | all-reduce | flops 512 | bytes 4096 | tf_op jit(solution)/shard_map/psum | solution.py:33
  85.8 39.6 %all-reduce = (f32[64,64]{0,1:T(8,128)S(1)}, f32[64,64]{0,1:T(8,128)S(1)}) all-reduce(f32[64,64]{0,1:T(8,128)S(1)} %fusion.18, f32[64,64]{0,1:T(8,128)S(1)} %fusion.20), channel_id=1, replica_groups=mesh['ia'=8,'ja'=2,'ka'=2] {'ia','ja','ka'}, use_global_device_ids=true, to_apply=%region_0.0 | all-reduce | flops 8192 | bytes 65536 | tf_op jit(solution)/shard_map/psum | solution.py:34
  125.5 5.8 %cholesky.44 = f32[64,64]{1,0:T(8,128)S(1)} custom-call(f32[64,64]{1,0:T(8,128)S(1)} %fusion.17), custom_call_target="Cholesky" | custom-call | tf_op jit(solution)/shard_map/jit(cholesky)/cholesky | solution.py:10
  131.4 0.6 compare_reduce_fusion.1
  132.0 0.7 fusion.5
  132.7 4.9 %custom-call.16 = f32[1,64,64]{1,2,0:T(8,128)S(1)} custom-call(f32[1,64,64]{2,1,0:T(8,128)S(1)} %fusion.5), custom_call_target="InvertDiagBlocksLowerTriangular" | custom-call | tf_op jit(solution)/shard_map/jit(_cho_solve)/triangular_solve | solution.py:11
  137.6 0.3 fusion.15
  137.9 0.2 multiply_reduce_fusion.1
  138.1 21.1 %psum.45 = f32[64]{0:T(128)S(1)} all-reduce(f32[64]{0:T(128)S(1)} %get-tuple-element.7), channel_id=1, replica_groups=mesh['ia'=8,'ja'=2,'ka'=2] {'ia'}, use_global_device_ids=true, to_apply=%region_6.8 | all-reduce | flops 64 | bytes 512 | tf_op jit(solution)/shard_map/psum | solution.py:37
  159.2 0.1 copy.21
  159.3 0.8 fusion.1
  160.1 1.0 copy.25
  161.1 0.2 fusion.22
  161.4 33.0 %psum.46 = f32[64,64]{0,1:T(8,128)S(1)} all-reduce(f32[64,64]{0,1:T(8,128)S(1)} %fusion.22), channel_id=1, replica_groups=mesh['ia'=8,'ja'=2,'ka'=2] {'ia'}, use_global_device_ids=true, to_apply=%region_7.9 | all-reduce | flops 4096 | bytes 32768 | tf_op jit(solution)/shard_map/psum | solution.py:39
  194.5 5.8 %cholesky.55 = f32[64,64]{1,0:T(8,128)S(1)} custom-call(f32[64,64]{1,0:T(8,128)S(1)} %fusion.11), custom_call_target="Cholesky" | custom-call | tf_op jit(solution)/shard_map/jit(cholesky)/cholesky | solution.py:10
  200.4 0.6 compare_reduce_fusion
  201.0 0.7 fusion.6
  201.7 4.9 %custom-call.17 = f32[1,64,64]{1,2,0:T(8,128)S(1)} custom-call(f32[1,64,64]{2,1,0:T(8,128)S(1)} %fusion.6), custom_call_target="InvertDiagBlocksLowerTriangular" | custom-call | tf_op jit(solution)/shard_map/jit(_cho_solve)/triangular_solve | solution.py:11
  206.6 27.3 %reduce-scatter.4.cloned.1.call-done = f32[64,64]{1,0:T(8,128)} async-done(((f32[1024,64]{1,0:T(8,128)}), f32[64,64]{1,0:T(8,128)}) %reduce-scatter.4.cloned.1.call-update) | async-done | bytes 16400
  233.9 1.0 fusion.9
  234.9 0.2 multiply_reduce_fusion
  235.1 36.9 %psum.47 = f32[64]{0:T(128)S(1)} all-reduce(f32[64]{0:T(128)S(1)} %get-tuple-element.9), channel_id=1, replica_groups=mesh['ia'=8,'ja'=2,'ka'=2] {'ia','ja','ka'}, use_global_device_ids=true, to_apply=%region_10.12 | all-reduce | flops 64 | bytes 512 | tf_op jit(solution)/shard_map/psum | solution.py:48
  272.0 0.6 multiply_bitcast_fusion
  (17 shorter events, 0.3 us)
Async XLA Ops:
  7.2 65.0 %copy-start = (bf16[8,1024,128]{2,1,0:T(8,128)(2,1)S(1)}, bf16[8,1024,128]{2,1,0:T(8,128)(2,1)}, u32[]{:S(2)}) copy-start(bf16[8,1024,128]{2,1,0:T(8,128)(2,1)} %param.4) | copy-start | bytes 6291460
  7.2 226.7 %reduce-scatter.4.cloned.1.call-start = ((), (), s32[]{:S(2)}) async-start(), calls=%async_computation.1 | async-start | bytes 557056
  159.2 113.4 %copy-start.1 = (f32[8,64]{1,0:T(8,128)}, f32[8,64]{1,0:T(8,128)S(1)}, u32[]{:S(2)}) copy-start(f32[8,64]{1,0:T(8,128)S(1)} %get-tuple-element.6) | copy-start | bytes 6148
Sparse Core Ops, SparseCore 0:
  161.2 72.5 reduce-scatter.3
where the time goes:
time: 281 us; the launch traced here: 279 us
  blocking collectives  203 us (72%)
  waiting for transfers between devices  27.3 us (10%)
  other arithmetic  26.4 us (9%)
  between operations  14.2 us (5%)
  matrix products  6.55 us (2%)
    all_gather x1, blocking collectives, body(): lax.all_gather(own_b.astype(jnp.bfloat16), ('ia', 'ka'), axis=0, tiled=True)  43.8 us
    psum x1, blocking collectives, body(): lax.psum((self_gram(own_b), self_gram(own_c)), ('ia', 'ja', 'ka'))  39.6 us
    psum x1, blocking collectives, body(): sums_b = lax.psum(jnp.sum(b_new * b_new, axis=0), ('ia', 'ja', 'ka'))  36.9 us
    psum x1, blocking collectives, body(): gram_a = lax.psum(self_gram(factor_a), 'ia')  33 us
    unnamed x2, waiting for transfers between devices  27.3 us
    psum x1, blocking collectives, body(): squares = lax.psum(jnp.sum(a_new * a_new, axis=0), 'ia')  21.1 us
    all_gather x1, blocking collectives, body(): lax.all_gather(own_c.astype(jnp.bfloat16), ('ia', 'ja'), axis=0, tiled=True)  17.2 us
    another operation x6, other arithmetic, solve_normal(): factor_low = jnp.linalg.cholesky(gram_mat)  13 us
  transfers between devices with their start and end apart: 1, of which 1 were waited for; matrix products, arithmetic and copies ran while one was open for 4% of the time, Pallas kernels for 0%

commit v1 on v0

v1 whole, which is shorter than its diff:
```python
import functools

import jax
import jax.numpy as jnp
from jax import lax
from jax.experimental import pallas as pl
from jax.experimental.pallas import tpu as pltpu
from jax.sharding import PartitionSpec as P

epsilon = 1e-06
HIGHEST = lax.Precision.HIGHEST
MESH = pl.DeviceIdType.MESH
f32 = jnp.float32
bf16 = jnp.bfloat16


def solve_normal(gram_mat, rhs_rows):
    factor_low = jnp.linalg.cholesky(gram_mat)
    return jax.scipy.linalg.cho_solve((factor_low, True), rhs_rows.T).T


def self_gram(rows_data):
    return jnp.dot(rows_data.T, rows_data, precision=HIGHEST, preferred_element_type=f32)


def body(tensor, factor_b, factor_c):
    rank_cols = factor_b.shape[-1]
    own_b = factor_b.reshape(-1, rank_cols)
    own_c = factor_c.reshape(-1, rank_cols)
    rows_i, rows_j, rows_k = tensor.shape
    block_c = lax.all_gather(own_c.astype(bf16), ("ia", "ja"), axis=0, tiled=True)
    partial_value = jnp.einsum("ijk,kr->irj", tensor, block_c, preferred_element_type=f32).astype(bf16)
    block_b = lax.all_gather(own_b.astype(bf16), ("ia", "ka"), axis=0, tiled=True)
    mode_local = jnp.einsum("irj,jr->ir", partial_value, block_b, preferred_element_type=f32)
    mode_a = lax.psum(mode_local, ("ja", "ka"))
    gram_b, gram_c = lax.psum((self_gram(own_b), self_gram(own_c)), ("ia", "ja", "ka"))
    a_new = solve_normal(gram_b * gram_c, mode_a)
    count_i = rows_i * lax.axis_size("ia")
    squares = lax.psum(jnp.sum(a_new * a_new, axis=0), "ia")
    factor_a = a_new * lax.rsqrt(squares / count_i + epsilon)
    gram_a = lax.psum(self_gram(factor_a), "ia")
    cast_a = factor_a.astype(bf16)
    mode_b = lax.psum_scatter(
        jnp.einsum("irj,ir->jr", partial_value, cast_a, preferred_element_type=f32),
        ("ia", "ka"),
        scatter_dimension=0,
        tiled=True,
    )
    b_new = solve_normal(gram_a * gram_c, mode_b)
    sums_b = lax.psum(jnp.sum(b_new * b_new, axis=0), ("ia", "ja", "ka"))
    count_j = rows_j * lax.axis_size("ja")
    out_rows = b_new * lax.rsqrt(sums_b / count_j + epsilon)
    return (factor_a, out_rows.reshape(factor_b.shape))


def dot0(a, b):
    return lax.dot_general(a, b, (((0,), (0,)), ((), ())), precision=HIGHEST, preferred_element_type=f32)


def sweep_inverse(mat, rank):
    lane = lax.rem(lax.broadcasted_iota(jnp.int32, mat.shape, 1), rank)
    row_id = lax.broadcasted_iota(jnp.int32, mat.shape, 0)
    for k in range(rank):
        col = jnp.broadcast_to(mat[:, k : k + 1], mat.shape)
        inv = 1.0 / col[k : k + 1, :]
        row = mat[k : k + 1, :] * inv
        row_new = jnp.where(lane[k : k + 1, :] == k, -inv, row)
        new = jnp.where(lane == k, col * inv, mat - col * row)
        mat = jnp.where(row_id == k, row_new, new)
    return -mat


def kernel(
    dims, x_hbm, b_ref, c_ref, fa_out, fb_out,
    xv, yv, bbuf, cbuf, bq, gbs, gcs, mabuf, fas, mbs, mbr, sbuf,
    x_sem, send, recv,
):
    ni, nj, nk = dims
    pi, pj, pk = lax.axis_index("ia"), lax.axis_index("ja"), lax.axis_index("ka")
    n_b, n_c, n_all = ni * nk, ni * nj, ni * nj * nk
    slot_b, slot_c = pi * nk + pk, pi * nj + pj
    me = (pi * nj + pj) * nk + pk
    rows_i, rows_j, _ = xv.shape
    rank = b_ref.shape[-1]
    half = b_ref.shape[0] // 2
    rows_c = c_ref.shape[0]

    def dev_b(t):
        return (t // nk, pj, lax.rem(t, nk))

    def dev_c(t):
        return (t // nj, lax.rem(t, nj), pk)

    def dev_all(t):
        return (t // (nj * nk), lax.rem(t // nk, nj), lax.rem(t, nk))

    def copy_to(src, dst, s, dev):
        return pltpu.make_async_remote_copy(
            src_ref=src, dst_ref=dst, send_sem=send.at[s], recv_sem=recv.at[s], device_id=dev, device_id_type=MESH
        )

    def spread(buf, s, mine, n, dev):
        def step(d, carry):
            copy_to(buf.at[mine], buf.at[mine], s, dev(lax.rem(mine + d, n))).start()
            return carry

        lax.fori_loop(1, n, step, 0)

    def all_of(buf, s, n, dev):
        rest = buf.at[pl.ds(0, n - 1)]
        return copy_to(rest, rest, s, dev(0))

    load_x = pltpu.make_async_copy(x_hbm, xv, x_sem)
    load_x.start()

    barrier = pltpu.get_barrier_semaphore()

    def greet(d, carry):
        pl.semaphore_signal(barrier, inc=1, device_id=dev_all(lax.rem(me + d, n_all)), device_id_type=MESH)
        return carry

    lax.fori_loop(1, n_all, greet, 0)

    own_b = b_ref[...]
    own_c = c_ref[...]
    bbuf[slot_b] = jnp.concatenate([own_b[:half], own_b[half:]], axis=1)
    cbuf[slot_c] = jnp.concatenate([own_c, own_c], axis=1)

    pl.semaphore_wait(barrier, n_all - 1)

    spread(cbuf, 0, slot_c, n_c, dev_c)
    spread(bbuf, 1, slot_b, n_b, dev_b)

    all_of(cbuf, 0, n_c, dev_c).wait_recv()
    c_all = cbuf[...].reshape(n_c * rows_c, 2 * rank)
    low = lax.broadcasted_iota(jnp.int32, c_all.shape, 1) < rank
    zero = jnp.zeros_like(c_all)
    c_two = jnp.concatenate([jnp.where(low, c_all, zero), jnp.where(low, zero, c_all)], axis=0).astype(bf16)
    gcs[pk] = dot0(c_all, c_all)[:rank]

    def send_gc(d, carry):
        copy_to(gcs.at[pk], gcs.at[pk], 2, (pi, pj, lax.rem(pk + d, nk))).start()
        return carry

    lax.fori_loop(1, nk, send_gc, 0)
    load_x.wait()

    def make_y(i, carry):
        x = xv[i].reshape(n_b, 2 * half, xv.shape[2])
        left = x[:, :half].reshape(n_b * half, xv.shape[2])
        right = x[:, half:].reshape(n_b * half, xv.shape[2])
        y = jnp.dot(jnp.concatenate([left, right], axis=1), c_two, preferred_element_type=f32)
        yv[i] = y.astype(bf16)
        return carry

    lax.fori_loop(0, rows_i, make_y, 0)

    all_of(bbuf, 1, n_b, dev_b).wait_recv()
    b_all = bbuf[...].reshape(n_b * half, 2 * rank)
    gram = dot0(b_all, b_all)
    low = lax.broadcasted_iota(jnp.int32, (rank, 2 * rank), 1) < rank
    gram = jnp.where(low, gram[:rank], gram[rank:])
    gbs[pj] = gram + pltpu.roll(gram, rank, 1)

    def send_gb(d, carry):
        copy_to(gbs.at[pj], gbs.at[pj], 3, (pi, lax.rem(pj + d, nj), pk)).start()
        return carry

    lax.fori_loop(1, nj, send_gb, 0)
    bq[...] = b_all.astype(bf16).astype(f32)

    def make_ma(i, carry):
        mabuf[me, pl.ds(i, 1), :] = jnp.sum(yv[i].astype(f32) * bq[...], axis=0, keepdims=True)
        return carry

    lax.fori_loop(0, rows_i, make_ma, 0)
    spread(mabuf, 4, me, n_all, dev_all)

    all_of(gcs, 2, nk, dev_b).wait_recv()
    all_of(gbs, 3, nj, dev_b).wait_recv()
    gram_c = jnp.sum(gcs[...], axis=0)
    inv_a = sweep_inverse(jnp.sum(gbs[...], axis=0) * gram_c, rank)

    all_of(mabuf, 4, n_all, dev_all).wait_recv()
    mode_a = jnp.sum(mabuf[...].reshape(ni, nj * nk, rows_i, 2 * rank), axis=1).reshape(ni * rows_i, 2 * rank)
    a_new = jnp.dot(
        mode_a, jnp.concatenate([inv_a, inv_a], axis=0), precision=HIGHEST, preferred_element_type=f32
    )
    squares = jnp.sum(a_new * a_new, axis=0, keepdims=True)
    factor_a = a_new * lax.rsqrt(squares / (ni * rows_i) + epsilon)
    fas[...] = factor_a
    own_a = fas[pl.ds(pl.multiple_of(pi * rows_i, rows_i), rows_i), :]
    fa_out[...] = own_a[:, :rank]
    cast_a = own_a.astype(bf16).astype(f32)

    def make_mb(d, carry):
        t = lax.rem(slot_b + d, n_b)
        rows = pl.ds(pl.multiple_of(t * half, half), half)
        total = yv[0, rows, :].astype(f32) * cast_a[0:1]
        for i in range(1, rows_i):
            total += yv[i, rows, :].astype(f32) * cast_a[i : i + 1]
        mbs[t] = total

        copy_to(mbs.at[t], mbr.at[slot_b], 5, dev_b(t)).start()
        return carry

    lax.fori_loop(1, n_b, make_mb, 0)
    rows = pl.ds(pl.multiple_of(slot_b * half, half), half)
    total = yv[0, rows, :].astype(f32) * cast_a[0:1]
    for i in range(1, rows_i):
        total += yv[i, rows, :].astype(f32) * cast_a[i : i + 1]
    mbr[slot_b] = total

    gram_a = dot0(factor_a, factor_a)[:rank]
    inv_b = sweep_inverse(gram_a * gram_c, rank)
    zero = jnp.zeros_like(inv_b)
    inv_two = jnp.concatenate([jnp.where(low, inv_b, zero), jnp.where(low, zero, inv_b)], axis=0)

    all_of(mbr, 5, n_b, dev_b).wait_recv()
    mode_b = jnp.sum(mbr[...], axis=0)
    b_new = jnp.dot(mode_b, inv_two, precision=HIGHEST, preferred_element_type=f32)
    sbuf[me] = jnp.sum(b_new * b_new, axis=0, keepdims=True)
    spread(sbuf, 6, me, n_all, dev_all)

    all_of(cbuf, 0, n_c, dev_c).wait_send()
    all_of(bbuf, 1, n_b, dev_b).wait_send()
    all_of(gcs, 2, nk, dev_b).wait_send()
    all_of(gbs, 3, nj, dev_b).wait_send()
    all_of(mabuf, 4, n_all, dev_all).wait_send()
    all_of(mbr, 5, n_b, dev_b).wait_send()

    all_of(sbuf, 6, n_all, dev_all).wait_recv()
    sums = jnp.broadcast_to(jnp.sum(sbuf[...], axis=0), (8, 2 * rank))
    sums = (sums + pltpu.roll(sums, rank, 1))[0:1]
    out = b_new * lax.rsqrt(sums / (nj * rows_j) + epsilon)
    fb_out[0:half, :] = out[:, :rank]
    fb_out[half:, :] = out[:, rank:]
    all_of(sbuf, 6, n_all, dev_all).wait_send()


def fused(dims, tensor, factor_b, factor_c):
    ni, nj, nk = dims
    rank = factor_b.shape[-1]
    own_b = factor_b.reshape(-1, rank)
    own_c = factor_c.reshape(-1, rank)
    rows_i, rows_j, rows_k = tensor.shape
    half = own_b.shape[0] // 2
    n_b, n_c, n_all = ni * nk, ni * nj, ni * nj * nk
    wide = 2 * rank
    vmem = pl.BlockSpec(memory_space=pltpu.VMEM)
    fa, fb = pl.pallas_call(
        functools.partial(kernel, dims),
        out_shape=(
            jax.ShapeDtypeStruct((rows_i, rank), f32),
            jax.ShapeDtypeStruct(own_b.shape, f32),
        ),
        in_specs=[pl.BlockSpec(memory_space=pl.ANY), vmem, vmem],
        out_specs=(vmem, vmem),
        scratch_shapes=[
            pltpu.VMEM(tensor.shape, bf16),
            pltpu.VMEM((rows_i, n_b * half, wide), bf16),
            pltpu.VMEM((n_b, half, wide), f32),
            pltpu.VMEM((n_c, own_c.shape[0], wide), f32),
            pltpu.VMEM((n_b * half, wide), f32),
            pltpu.VMEM((nj, rank, wide), f32),
            pltpu.VMEM((nk, rank, wide), f32),
            pltpu.VMEM((n_all, rows_i, wide), f32),
            pltpu.VMEM((ni * rows_i, wide), f32),
            pltpu.VMEM((n_b, half, wide), f32),
            pltpu.VMEM((n_b, half, wide), f32),
            pltpu.VMEM((n_all, 1, wide), f32),
            pltpu.SemaphoreType.DMA,
            pltpu.SemaphoreType.DMA((7,)),
            pltpu.SemaphoreType.DMA((7,)),
        ],
        compiler_params=pltpu.CompilerParams(
            collective_id=0, has_side_effects=True, vmem_limit_bytes=63 * 1024 * 1024
        ),
    )(tensor, own_b, own_c)
    return fa, fb.reshape(factor_b.shape)


def solution(mesh):
    dims = tuple(mesh.shape[a] for a in ("ia", "ja", "ka"))

    def step(tensor, factor_b, factor_c):
        whole_tiles = (
            factor_b.shape[-2] % 32 == 0
            and factor_c.shape[-2] % 8 == 0
            and tensor.shape[0] % 8 == 0
            and factor_b.shape[-1] == 64
        )
        if whole_tiles:
            return fused(dims, tensor, factor_b, factor_c)
        return body(tensor, factor_b, factor_c)

    return jax.shard_map(
        step,
        mesh=mesh,
        in_specs=(
            P("ia", "ja", "ka"),
            P("ia", "ja", "ka", None, None),
            P("ka", "ia", "ja", None, None),
        ),
        out_specs=(P("ia", None), P("ia", "ja", "ka", None, None)),
        check_vma=False,
    )
```

time: 281 us -> 41.6 us (0.15)
  blocking collectives: 203 us -> 0 us
  Pallas kernels: 0 us -> 38 us
  waiting for transfers between devices: 27.3 us -> 0 us
  other arithmetic: 26.4 us -> 0 us
  between operations: 14.2 us -> 0.64 us
  matrix products: 6.55 us -> 0 us
    psum x5 -> x0, blocking collectives: 142 us -> none  [the longest x1 39.6 us: body(): lax.psum((self_gram(own_b), self_gram(own_c)), ('ia', 'ja', 'ka'))]
    all_gather x2 -> x0, blocking collectives: 61 us -> none  [the longest x1 43.8 us: body(): lax.all_gather(own_b.astype(jnp.bfloat16), ('ia', 'ka'), axis=0, tiled=True)]
    pallas_call x0 -> x1, Pallas kernels: none -> 38 us  [fused(): pl.pallas_call(functools.partial(kernel, dims), out_shape=(jax.ShapeDtype...]
    unnamed x2 -> x0, waiting for transfers between devices: 27.3 us -> none
    another operation x10 -> x0, other arithmetic: 24.1 us -> none  [the longest x6 13 us: solve_normal(): factor_low = jnp.linalg.cholesky(gram_mat)]
    dot_general x6 -> x0, matrix products: 4.85 us -> none  [the longest x3 2.29 us: self_gram(): jnp.dot(rows_data.T, rows_data, precision=lax.Precision.HIGHEST, preferre...]
  transfers between devices with their start and end apart: 1 -> 0, of which waited for: 1 -> 0; matrix products, arithmetic and copies ran while one was open for 4% -> 0% of each run, Pallas kernels for 0% -> 0%
where the time goes in v1:
time: 41.6 us; the launch traced here: 41.3 us
  Pallas kernels  38 us (91%)
  local copies, waits for them, and re-layouts  2.65 us (6%)
  between operations  0.64 us (2%)
    pallas_call x1, Pallas kernels, fused(): pl.pallas_call(functools.partial(kernel, dims), out_shape=(jax.ShapeDtype...  38 us
    unnamed x2, local copies, waits for them, and re-layouts  2.65 us

profile of v1, /device:TPU:0, one launch (start us, length us, event | category | flops | bytes accessed | tf_op | source)
XLA Modules:
  0.0 41.3 jit_solution(2501773763043174708)
XLA Ops:
  0.6 38.0 %shard_map.50 = (f32[8,64]{1,0:T(8,128)}, f32[64,64]{1,0:T(8,128)}) custom-call(bf16[8,1024,128]{2,1,0:T(8,128)(2,1)} %x_hbm.1, f32[64,64]{1,0:T(8,128)} %bitcast.3, f32[8,64]{1,0:T(8,128)} %bitcast.5), custom_call_target="tpu_custom_call" | custom-call | tf_op jit(solution)/shard_map/pallas_call | solution.py:251
  38.6 1.3 %copy.7 = f32[8,64]{1,0:T(8,128)} copy(f32[8,64]{1,0:T(8,128)} %get-tuple-element.8) | data formatting | bytes 4096
  39.9 1.4 %copy.8 = f32[1,1,1,64,64]{4,3,2,1,0:T(8,128)} copy(f32[1,1,1,64,64]{4,3,2,1,0:T(8,128)} %bitcast.4) | data formatting | bytes 32768

commit v2 on v1

--- a/solution.py
+++ b/solution.py
@@ -72,7 +72,7 @@
 
 def kernel(
     dims, x_hbm, b_ref, c_ref, fa_out, fb_out,
-    xv, yv, bbuf, cbuf, bq, gbs, gcs, mabuf, fas, mbs, mbr, sbuf,
+    xv, yv, bhi, blo, cbuf, bq, gbs, gcs, mas, mabuf, fas, mbs, mbr, sbuf,
     x_sem, send, recv,
 ):
     ni, nj, nk = dims
@@ -123,13 +123,17 @@
 
     own_b = b_ref[...]
     own_c = c_ref[...]
-    bbuf[slot_b] = jnp.concatenate([own_b[:half], own_b[half:]], axis=1)
+    wide_b = jnp.concatenate([own_b[:half], own_b[half:]], axis=1)
+    high_b = wide_b.astype(bf16)
+    bhi[slot_b] = high_b
+    blo[slot_b] = (wide_b - high_b.astype(f32)).astype(bf16)
     cbuf[slot_c] = jnp.concatenate([own_c, own_c], axis=1)
 
     pl.semaphore_wait(barrier, n_all - 1)
 
     spread(cbuf, 0, slot_c, n_c, dev_c)
-    spread(bbuf, 1, slot_b, n_b, dev_b)
+    spread(bhi, 1, slot_b, n_b, dev_b)
+    spread(blo, 7, slot_b, n_b, dev_b)
 
     all_of(cbuf, 0, n_c, dev_c).wait_recv()
     c_all = cbuf[...].reshape(n_c * rows_c, 2 * rank)
@@ -155,8 +159,21 @@
 
     lax.fori_loop(0, rows_i, make_y, 0)
 
-    all_of(bbuf, 1, n_b, dev_b).wait_recv()
-    b_all = bbuf[...].reshape(n_b * half, 2 * rank)
+    all_of(bhi, 1, n_b, dev_b).wait_recv()
+    bq[...] = bhi[...].reshape(n_b * half, 2 * rank).astype(f32)
+
+    def make_ma(i, carry):
+        mas[pl.ds(i, 1), :] = jnp.sum(yv[i].astype(f32) * bq[...], axis=0, keepdims=True)
+        return carry
+
+    lax.fori_loop(0, rows_i, make_ma, 0)
+    part = mas[...] + pltpu.roll(mas[...], rank, 1)
+    low = lax.broadcasted_iota(jnp.int32, (rows_i // 2, 2 * rank), 1) < rank
+    mabuf[me] = jnp.where(low, part[: rows_i // 2], part[rows_i // 2 :])
+    spread(mabuf, 4, me, n_all, dev_all)
+
+    all_of(blo, 7, n_b, dev_b).wait_recv()
+    b_all = bq[...] + blo[...].reshape(n_b * half, 2 * rank).astype(f32)
     gram = dot0(b_all, b_all)
     low = lax.broadcasted_iota(jnp.int32, (rank, 2 * rank), 1) < rank
     gram = jnp.where(low, gram[:rank], gram[rank:])
@@ -167,14 +184,6 @@
         return carry
 
     lax.fori_loop(1, nj, send_gb, 0)
-    bq[...] = b_all.astype(bf16).astype(f32)
-
-    def make_ma(i, carry):
-        mabuf[me, pl.ds(i, 1), :] = jnp.sum(yv[i].astype(f32) * bq[...], axis=0, keepdims=True)
-        return carry
-
-    lax.fori_loop(0, rows_i, make_ma, 0)
-    spread(mabuf, 4, me, n_all, dev_all)
 
     all_of(gcs, 2, nk, dev_b).wait_recv()
     all_of(gbs, 3, nj, dev_b).wait_recv()
@@ -182,7 +191,11 @@
     inv_a = sweep_inverse(jnp.sum(gbs[...], axis=0) * gram_c, rank)
 
     all_of(mabuf, 4, n_all, dev_all).wait_recv()
-    mode_a = jnp.sum(mabuf[...].reshape(ni, nj * nk, rows_i, 2 * rank), axis=1).reshape(ni * rows_i, 2 * rank)
+    mode_a = jnp.sum(mabuf[...].reshape(ni, nj * nk, rows_i // 2, 2 * rank), axis=1)
+    first = lax.broadcasted_iota(jnp.int32, mode_a.shape, 2) < rank
+    zero = jnp.zeros_like(mode_a)
+    mode_a = jnp.concatenate([jnp.where(first, mode_a, zero), jnp.where(first, zero, mode_a)], axis=1)
+    mode_a = mode_a.reshape(ni * rows_i, 2 * rank)
     a_new = jnp.dot(
         mode_a, jnp.concatenate([inv_a, inv_a], axis=0), precision=HIGHEST, preferred_element_type=f32
     )
@@ -199,7 +212,7 @@
         total = yv[0, rows, :].astype(f32) * cast_a[0:1]
         for i in range(1, rows_i):
             total += yv[i, rows, :].astype(f32) * cast_a[i : i + 1]
-        mbs[t] = total
+        mbs[t] = total.astype(bf16)
 
         copy_to(mbs.at[t], mbr.at[slot_b], 5, dev_b(t)).start()
         return carry
@@ -209,7 +222,7 @@
     total = yv[0, rows, :].astype(f32) * cast_a[0:1]
     for i in range(1, rows_i):
         total += yv[i, rows, :].astype(f32) * cast_a[i : i + 1]
-    mbr[slot_b] = total
+    mbr[slot_b] = total.astype(bf16)
 
     gram_a = dot0(factor_a, factor_a)[:rank]
     inv_b = sweep_inverse(gram_a * gram_c, rank)
@@ -217,13 +230,14 @@
     inv_two = jnp.concatenate([jnp.where(low, inv_b, zero), jnp.where(low, zero, inv_b)], axis=0)
 
     all_of(mbr, 5, n_b, dev_b).wait_recv()
-    mode_b = jnp.sum(mbr[...], axis=0)
+    mode_b = jnp.sum(mbr[...].astype(f32), axis=0)
     b_new = jnp.dot(mode_b, inv_two, precision=HIGHEST, preferred_element_type=f32)
     sbuf[me] = jnp.sum(b_new * b_new, axis=0, keepdims=True)
     spread(sbuf, 6, me, n_all, dev_all)
 
     all_of(cbuf, 0, n_c, dev_c).wait_send()
-    all_of(bbuf, 1, n_b, dev_b).wait_send()
+    all_of(bhi, 1, n_b, dev_b).wait_send()
+    all_of(blo, 7, n_b, dev_b).wait_send()
     all_of(gcs, 2, nk, dev_b).wait_send()
     all_of(gbs, 3, nj, dev_b).wait_send()
     all_of(mabuf, 4, n_all, dev_all).wait_send()
@@ -236,6 +250,15 @@
     fb_out[0:half, :] = out[:, :rank]
     fb_out[half:, :] = out[:, rank:]
     all_of(sbuf, 6, n_all, dev_all).wait_send()
+
+
+def place(a_ref, b_ref, a_out, b_out, sem):
+    first = pltpu.make_async_copy(a_ref, a_out, sem.at[0])
+    second = pltpu.make_async_copy(b_ref, b_out, sem.at[1])
+    second.start()
+    first.start()
+    second.wait()
+    first.wait()
 
 
 def fused(dims, tensor, factor_b, factor_c):
@@ -259,24 +282,33 @@
         scratch_shapes=[
             pltpu.VMEM(tensor.shape, bf16),
             pltpu.VMEM((rows_i, n_b * half, wide), bf16),
-            pltpu.VMEM((n_b, half, wide), f32),
+            pltpu.VMEM((n_b, half, wide), bf16),
+            pltpu.VMEM((n_b, half, wide), bf16),
             pltpu.VMEM((n_c, own_c.shape[0], wide), f32),
             pltpu.VMEM((n_b * half, wide), f32),
             pltpu.VMEM((nj, rank, wide), f32),
             pltpu.VMEM((nk, rank, wide), f32),
-            pltpu.VMEM((n_all, rows_i, wide), f32),
+            pltpu.VMEM((rows_i, wide), f32),
+            pltpu.VMEM((n_all, rows_i // 2, wide), f32),
             pltpu.VMEM((ni * rows_i, wide), f32),
-            pltpu.VMEM((n_b, half, wide), f32),
-            pltpu.VMEM((n_b, half, wide), f32),
+            pltpu.VMEM((n_b, half, wide), bf16),
+            pltpu.VMEM((n_b, half, wide), bf16),
             pltpu.VMEM((n_all, 1, wide), f32),
             pltpu.SemaphoreType.DMA,
-            pltpu.SemaphoreType.DMA((7,)),
-            pltpu.SemaphoreType.DMA((7,)),
+            pltpu.SemaphoreType.DMA((8,)),
+            pltpu.SemaphoreType.DMA((8,)),
         ],
         compiler_params=pltpu.CompilerParams(
             collective_id=0, has_side_effects=True, vmem_limit_bytes=63 * 1024 * 1024
         ),
     )(tensor, own_b, own_c)
+    fa, fb = pl.pallas_call(
+        place,
+        out_shape=(jax.ShapeDtypeStruct(fa.shape, f32), jax.ShapeDtypeStruct(fb.shape, f32)),
+        in_specs=[vmem, vmem],
+        out_specs=(pl.BlockSpec(memory_space=pl.ANY), pl.BlockSpec(memory_space=pl.ANY)),
+        scratch_shapes=[pltpu.SemaphoreType.DMA((2,))],
+    )(fa, fb)
     return fa, fb.reshape(factor_b.shape)
 
 

time: 41.6 us -> 38.3 us (0.921)
  local copies, waits for them, and re-layouts: 2.65 us -> 0 us
  Pallas kernels: 38 us -> 37.4 us
    unnamed x2 -> x0, local copies, waits for them, and re-layouts: 2.65 us -> none
    pallas_call x1, Pallas kernels: 38 us -> 36 us  [fused(): pl.pallas_call(functools.partial(kernel, dims), out_shape=(jax.ShapeDtype...]
    pallas_call x0 -> x1, Pallas kernels: none -> 1.4 us  [fused(): pl.pallas_call(place, out_shape=(jax.ShapeDtypeStruct(fa.shape, f32), jax...]
where the time goes in v2:
time: 38.3 us; the launch traced here: 38 us
  Pallas kernels  37.4 us (98%)
  between operations  0.64 us (2%)
    pallas_call x1, Pallas kernels, fused(): pl.pallas_call(functools.partial(kernel, dims), out_shape=(jax.ShapeDtype...  36 us
    pallas_call x1, Pallas kernels, fused(): pl.pallas_call(place, out_shape=(jax.ShapeDtypeStruct(fa.shape, f32), jax...  1.4 us

profile of v2, /device:TPU:0, one launch (start us, length us, event | category | flops | bytes accessed | tf_op | source)
XLA Modules:
  0.0 38.0 jit_solution(17859427644973270715)
XLA Ops:
  0.6 36.0 %shard_map.50 = (f32[8,64]{1,0:T(8,128)}, f32[64,64]{1,0:T(8,128)}) custom-call(bf16[8,1024,128]{2,1,0:T(8,128)(2,1)} %x_hbm.1, f32[64,64]{1,0:T(8,128)} %bitcast.3, f32[8,64]{1,0:T(8,128)} %bitcast.4), custom_call_target="tpu_custom_call" | custom-call | tf_op jit(solution)/shard_map/pallas_call | solution.py:274
  36.6 1.4 %shard_map.51 = (f32[8,64]{1,0:T(8,128)}, f32[64,64]{1,0:T(8,128)}) custom-call(f32[8,64]{1,0:T(8,128)} %get-tuple-element.6.a_ref, f32[64,64]{1,0:T(8,128)} %get-tuple-element.7.b_ref), custom_call_target="tpu_custom_call" | custom-call | tf_op jit(solution)/shard_map/pallas_call | solution.py:305

commit v3 on v2

--- a/solution.py
+++ b/solution.py
@@ -60,14 +60,27 @@
 def sweep_inverse(mat, rank):
     lane = lax.rem(lax.broadcasted_iota(jnp.int32, mat.shape, 1), rank)
     row_id = lax.broadcasted_iota(jnp.int32, mat.shape, 0)
-    for k in range(rank):
-        col = jnp.broadcast_to(mat[:, k : k + 1], mat.shape)
-        inv = 1.0 / col[k : k + 1, :]
-        row = mat[k : k + 1, :] * inv
-        row_new = jnp.where(lane[k : k + 1, :] == k, -inv, row)
-        new = jnp.where(lane == k, col * inv, mat - col * row)
-        mat = jnp.where(row_id == k, row_new, new)
-    return -mat
+    diag = jnp.where(lane == row_id, mat, 0.0)
+    scale = lax.rsqrt(jnp.sum(diag, axis=0, keepdims=True))
+    scale = lax.rsqrt(jnp.sum(diag[:, :rank], axis=1, keepdims=True)) * scale
+    mat = mat * scale
+    for k in range(0, rank, 2):
+        col1 = jnp.broadcast_to(mat[:, k : k + 1], mat.shape)
+        col2 = jnp.broadcast_to(mat[:, k + 1 : k + 2], mat.shape)
+        row1, row2 = mat[k : k + 1, :], mat[k + 1 : k + 2, :]
+        p11, p12, p22 = col1[k : k + 1, :], col2[k : k + 1, :], col2[k + 1 : k + 2, :]
+        inv = 1.0 / (p11 * p22 - p12 * p12)
+        q11, q12, q22 = p22 * inv, -p12 * inv, p11 * inv
+        new1 = q11 * row1 + q12 * row2
+        new2 = q12 * row1 + q22 * row2
+        new = mat - col1 * new1 - col2 * new2
+        new = jnp.where(lane == k, q11 * col1 + q12 * col2, new)
+        new = jnp.where(lane == k + 1, q12 * col1 + q22 * col2, new)
+        lane1 = lane[0:1, :]
+        new1 = jnp.where(lane1 == k, -q11, jnp.where(lane1 == k + 1, -q12, new1))
+        new2 = jnp.where(lane1 == k, -q12, jnp.where(lane1 == k + 1, -q22, new2))
+        mat = jnp.where(row_id == k, new1, jnp.where(row_id == k + 1, new2, new))
+    return -mat * scale
 
 
 def kernel(
@@ -127,7 +140,7 @@
     high_b = wide_b.astype(bf16)
     bhi[slot_b] = high_b
     blo[slot_b] = (wide_b - high_b.astype(f32)).astype(bf16)
-    cbuf[slot_c] = jnp.concatenate([own_c, own_c], axis=1)
+    cbuf[slot_c] = jnp.concatenate([own_c[: rows_c // 2], own_c[rows_c // 2 :]], axis=1)
 
     pl.semaphore_wait(barrier, n_all - 1)
 
@@ -136,10 +149,15 @@
     spread(blo, 7, slot_b, n_b, dev_b)
 
     all_of(cbuf, 0, n_c, dev_c).wait_recv()
-    c_all = cbuf[...].reshape(n_c * rows_c, 2 * rank)
-    low = lax.broadcasted_iota(jnp.int32, c_all.shape, 1) < rank
+    c_all = cbuf[...]
+    first = lax.broadcasted_iota(jnp.int32, c_all.shape, 2) < rank
     zero = jnp.zeros_like(c_all)
-    c_two = jnp.concatenate([jnp.where(low, c_all, zero), jnp.where(low, zero, c_all)], axis=0).astype(bf16)
+    c_odd = jnp.where(first, zero, c_all).reshape(n_c * rows_c // 2, 2 * rank)
+    c_odd = pltpu.roll(c_odd, rank, 1).reshape(c_all.shape)
+    c_left = jnp.concatenate([jnp.where(first, c_all, zero), c_odd], axis=1).reshape(n_c * rows_c, 2 * rank)
+    c_right = pltpu.roll(c_left, rank, 1)
+    c_two = jnp.concatenate([c_left, c_right], axis=0).astype(bf16)
+    c_all = c_left + c_right
     gcs[pk] = dot0(c_all, c_all)[:rank]
 
     def send_gc(d, carry):
@@ -284,7 +302,7 @@
             pltpu.VMEM((rows_i, n_b * half, wide), bf16),
             pltpu.VMEM((n_b, half, wide), bf16),
             pltpu.VMEM((n_b, half, wide), bf16),
-            pltpu.VMEM((n_c, own_c.shape[0], wide), f32),
+            pltpu.VMEM((n_c, own_c.shape[0] // 2, wide), f32),
             pltpu.VMEM((n_b * half, wide), f32),
             pltpu.VMEM((nj, rank, wide), f32),
             pltpu.VMEM((nk, rank, wide), f32),

time: 38.3 us -> 34.5 us (0.901)
  Pallas kernels: 37.4 us -> 33.6 us
    pallas_call x1, Pallas kernels: 36 us -> 32.2 us  [fused(): pl.pallas_call(functools.partial(kernel, dims), out_shape=(jax.ShapeDtype...]
where the time goes in v3:
time: 34.5 us; the launch traced here: 34.2 us
  Pallas kernels  33.6 us (97%)
  between operations  0.64 us (2%)
    pallas_call x1, Pallas kernels, fused(): pl.pallas_call(functools.partial(kernel, dims), out_shape=(jax.ShapeDtype...  32.2 us
    pallas_call x1, Pallas kernels, fused(): pl.pallas_call(place, out_shape=(jax.ShapeDtypeStruct(fa.shape, f32), jax...  1.4 us

profile of v3, /device:TPU:0, one launch (start us, length us, event | category | flops | bytes accessed | tf_op | source)
XLA Modules:
  0.0 34.2 jit_solution(698435492066798610)
XLA Ops:
  0.6 32.2 %shard_map.50 = (f32[8,64]{1,0:T(8,128)}, f32[64,64]{1,0:T(8,128)}) custom-call(bf16[8,1024,128]{2,1,0:T(8,128)(2,1)} %x_hbm.1, f32[64,64]{1,0:T(8,128)} %bitcast.3, f32[8,64]{1,0:T(8,128)} %bitcast.4), custom_call_target="tpu_custom_call" | custom-call | tf_op jit(solution)/shard_map/pallas_call | solution.py:292
  32.8 1.4 %shard_map.51 = (f32[8,64]{1,0:T(8,128)}, f32[64,64]{1,0:T(8,128)}) custom-call(f32[8,64]{1,0:T(8,128)} %get-tuple-element.6.a_ref, f32[64,64]{1,0:T(8,128)} %get-tuple-element.7.b_ref), custom_call_target="tpu_custom_call" | custom-call | tf_op jit(solution)/shard_map/pallas_call | solution.py:323

commit v4 on v3

--- a/solution.py
+++ b/solution.py
@@ -146,7 +146,6 @@
 
     spread(cbuf, 0, slot_c, n_c, dev_c)
     spread(bhi, 1, slot_b, n_b, dev_b)
-    spread(blo, 7, slot_b, n_b, dev_b)
 
     all_of(cbuf, 0, n_c, dev_c).wait_recv()
     c_all = cbuf[...]
@@ -165,6 +164,7 @@
         return carry
 
     lax.fori_loop(1, nk, send_gc, 0)
+    spread(blo, 7, slot_b, n_b, dev_b)
     load_x.wait()
 
     def make_y(i, carry):

time: 34.5 us -> 34.9 us (1.012)
  Pallas kernels: 33.6 us -> 34 us
    pallas_call x1, Pallas kernels: 32.2 us -> 32.6 us  [fused(): pl.pallas_call(functools.partial(kernel, dims), out_shape=(jax.ShapeDtype...]
where the time goes in v4:
time: 34.9 us; the launch traced here: 34.6 us
  Pallas kernels  34 us (97%)
  between operations  0.64 us (2%)
    pallas_call x1, Pallas kernels, fused(): pl.pallas_call(functools.partial(kernel, dims), out_shape=(jax.ShapeDtype...  32.6 us
    pallas_call x1, Pallas kernels, fused(): pl.pallas_call(place, out_shape=(jax.ShapeDtypeStruct(fa.shape, f32), jax...  1.4 us

profile of v4, /device:TPU:0, one launch (start us, length us, event | category | flops | bytes accessed | tf_op | source)
XLA Modules:
  0.0 34.6 jit_solution(12656590579402648877)
XLA Ops:
  0.6 32.6 %shard_map.50 = (f32[8,64]{1,0:T(8,128)}, f32[64,64]{1,0:T(8,128)}) custom-call(bf16[8,1024,128]{2,1,0:T(8,128)(2,1)} %x_hbm.1, f32[64,64]{1,0:T(8,128)} %bitcast.3, f32[8,64]{1,0:T(8,128)} %bitcast.4), custom_call_target="tpu_custom_call" | custom-call | tf_op jit(solution)/shard_map/pallas_call | solution.py:292
  33.2 1.4 %shard_map.51 = (f32[8,64]{1,0:T(8,128)}, f32[64,64]{1,0:T(8,128)}) custom-call(f32[8,64]{1,0:T(8,128)} %get-tuple-element.6.a_ref, f32[64,64]{1,0:T(8,128)} %get-tuple-element.7.b_ref), custom_call_target="tpu_custom_call" | custom-call | tf_op jit(solution)/shard_map/pallas_call | solution.py:323
